TPU v7x, 32 devices: a whole 2x2x4 slice. The times are simulated.
32 devices in a mesh: groups: 2 (over y), batch: 16 (over z, x, core).
Axes of the slice: x: 2, y: 2, z: 4, core: 2. Of those that a mesh axis runs over, the one named last changes fastest.
Arguments:
- queries: bfloat16 [64, 34, 8192], P(('groups', 'batch')), parts along dimension 0, may hold values from -6 to 6
- key_vectors: bfloat16 [64, 34, 8192], P(('groups', 'batch')), parts along dimension 0, may hold values from -0.5 to 0.5
- values: bfloat16 [64, 34, 8192], P(('groups', 'batch')), parts along dimension 0, may hold values from -6 to 6
- gate_logits: bfloat16 [64, 34, 8192], P(('groups', 'batch')), parts along dimension 0, may hold values from -6 to 6
- decay_rates: float32 [64], replicated, may hold values from 0.003 to 0.08
- norm_gain: float32 [8192], replicated, may hold values from 0.1 to 1.9
- pool_states: bfloat16 [32, 8192, 128], P(('groups', 'batch')), parts along dimension 0, may hold values from -1.75 to 1.75
- pool_entry: int32 [64], P(('groups', 'batch')), parts along dimension 0, may hold values from 0 to 15
Outputs:
- mixed: bfloat16 [64, 34, 8192], P(('groups', 'batch')), parts along dimension 0
- new_states: bfloat16 [64, 8192, 128], P('groups', 'batch'), parts along dimension 0
There are 2 independent parts, one for each index of `groups`. A program takes and returns all parts, laid end to end along the dimension named above; an argument that names none is the same for every part. Nothing has to cross between parts.
Inputs may be any that keep to these rules, and one draw needn't show every extreme that they name: `pool_entry`: entry e is the only entry of the pool shard on batch device e; several requests may name the same entry.
All inputs are finite; a program needn't handle non-finite values.
Results may differ from a plain program's by a relative error of at most 0.001.
Values may be sent and summed in bfloat16 or wider, within the bound.
A program may use at most 64 MiB of HBM per device.

v0:
```python
import jax
import jax.numpy as jnp
from jax import lax
from jax.sharding import PartitionSpec as P


def finish_output(attended, gate_logits, norm_gain):
    mean_square = jnp.mean(attended * attended, axis=-1, keepdims=True)
    scaled = attended * lax.rsqrt(mean_square + 1e-05) * norm_gain
    return (scaled * jax.nn.sigmoid(gate_logits.astype(jnp.float32))).astype(jnp.bfloat16)


def attend(query_part, key_part, value_part, resumed, rates_here):
    length = query_part.shape[1]
    highest = lax.Precision.HIGHEST
    positions = jnp.arange(1, length + 1).astype(jnp.float32)
    decay_now = jnp.exp(-positions[:, None] * rates_here[None, :])
    from_state = jnp.einsum(
        "rtgd,rgde->rtge", query_part, resumed, preferred_element_type=jnp.float32
    )
    from_state = from_state * decay_now[None, :, :, None]
    key_wide = key_part.astype(jnp.float32)
    value_wide = value_part.astype(jnp.float32)
    distance = positions[:, None] - positions[None, :]
    decay_pair = jnp.where(
        (distance >= 0.0)[:, :, None],
        jnp.exp(-jnp.maximum(distance, 0.0)[:, :, None] * rates_here),
        0.0,
    )
    scores = (
        jnp.einsum("rtgd,rsgd->rtsg", query_part, key_part, preferred_element_type=jnp.float32)
        * decay_pair[None]
    )
    in_block = jnp.einsum("rtsg,rsge->rtge", scores, value_wide, precision=highest)
    tail_decay = jnp.exp(-(float(length) - positions)[:, None] * rates_here[None, :])
    weighted_keys = key_wide * tail_decay[None, :, :, None]
    updated = jnp.exp(-float(length) * rates_here)[None, :, None, None] * resumed.astype(
        jnp.float32
    )
    updated = updated + jnp.einsum("rsgd,rsge->rgde", weighted_keys, value_wide, precision=highest)
    return (from_state + in_block, updated)


def on_device(
    queries, key_vectors, values, gate_logits, decay_rates, norm_gain, pool_states, pool_entry
):
    req_dev, length, feature_width = queries.shape
    head_count = decay_rates.shape[0]
    head_size = pool_states.shape[2]
    entries = lax.all_gather(pool_entry, "batch", axis=0, tiled=True)
    spread = lax.all_to_all(pool_states, "batch", split_axis=1, concat_axis=0, tiled=True)
    chosen = jnp.take(spread, entries, axis=0)
    resumed = lax.all_to_all(chosen, "batch", split_axis=0, concat_axis=1, tiled=True)
    resumed = resumed.reshape(req_dev, head_count, head_size, head_size)
    shaped = (req_dev, length, head_count, head_size)
    attended, updated = attend(
        queries.reshape(shaped),
        key_vectors.reshape(shaped),
        values.reshape(shaped),
        resumed,
        decay_rates,
    )
    attended = attended.reshape(req_dev, length, feature_width)
    local_states = updated.astype(jnp.bfloat16).reshape(req_dev, feature_width, head_size)
    new_states = lax.all_to_all(local_states, "batch", split_axis=1, concat_axis=0, tiled=True)
    mixed = finish_output(attended, gate_logits, norm_gain)
    return (mixed, new_states)


def solution(mesh):
    placed = (
        P(("groups", "batch"), None, None),
        P(("groups", "batch"), None, None),
        P(("groups", "batch"), None, None),
        P(("groups", "batch"), None, None),
        P(),
        P(),
        P(("groups", "batch"), None, None),
        P(("groups", "batch")),
    )
    return jax.shard_map(
        on_device,
        mesh=mesh,
        in_specs=placed,
        out_specs=(P(("groups", "batch"), None, None), P("groups", "batch", None)),
        check_vma=False,
    )
```

profile of v0, /device:TPU:11, one launch (start us, length us, event | category | flops | bytes accessed | tf_op | source)
XLA Modules:
  0.0 375.5 jit_solution(9554630048918124368)
XLA Ops:
  0.6 7.5 %copy.67 = bf16[1,8192,128]{2,0,1:T(2,128)(2,1)} copy(bf16[1,8192,128]{2,1,0:T(8,128)(2,1)} %param.14) | data formatting | bytes 4194304 | tf_op args[6]
  8.6 45.2 %reduce.1 = bf16[8192,128]{1,0:T(8,128)(2,1)S(1)} reduce(bf16[8192,1,128]{2,1,0:T(2,128)(2,1)} %bitcast.38, bf16[]{:T(256)} %broadcast.157), dimensions={1}, to_apply=%bitcast.34.reduce_sub_computation | reduce | bytes 4194306
  53.8 2.0 reshape.201
  55.8 6.7 %all-to-all-start = ((bf16[16,2,32768]{2,1,0:T(2,128)(2,1)}), bf16[16,2,32768]{2,1,0:T(2,128)(2,1)S(1)}, u32[]{:S(2)}, u32[]{:S(2)}) async-start(bf16[16,2,32768]{2,1,0:T(2,128)(2,1)} %reshape.201), calls=%async_computation | async-start | bytes 4194304 | tf_op jit(solution)/shard_map/all_to_all | solution.py:51
  64.0 43.9 %all-reduce = s32[32]{0:T(128)S(1)} all-reduce(s32[32]{0:T(128)S(1)} %dynamic-update-slice), channel_id=1, replica_groups=mesh['groups'=2,'batch'=16] {'batch'}, use_global_device_ids=true, to_apply=%add | all-reduce | flops 32 | bytes 256
  107.9 2.1 all-to-all-done
  110.0 6.7 %reshape.202 = bf16[8192,1,128]{2,1,0:T(2,128)(2,1)} reshape(bf16[16,2,32768]{2,1,0:T(2,128)(2,1)S(1)} %all-to-all-done) | data formatting | bytes 4194304
  116.8 2.5 copy.49
  119.2 3.1 gather_fusion
  122.3 4.7 %broadcast_select_fusion = bf16[32,512,128]{2,1,0:T(8,128)(2,1)} fusion(bf16[32,512,128]{2,1,0:T(8,128)(2,1)} %gather_fusion, pred[32]{0:T(512)(128)(4,1)S(1)} %compare_and_fusion), kind=kLoop, calls=%fused_computation.2 | loop fusion | flops 2097152 | bytes 8388640 | tf_op jit(solution)/shard_map/jit(_take)/select_n | solution.py:52
  127.0 6.3 %all-to-all-start.1 = ((bf16[32,512,128]{2,1,0:T(8,128)(2,1)}), bf16[32,512,128]{2,1,0:T(8,128)(2,1)}, u32[]{:S(2)}, u32[]{:S(2)}) async-start(bf16[32,512,128]{2,1,0:T(8,128)(2,1)} %broadcast_select_fusion), calls=%async_computation.1 | async-start | bytes 8388608 | tf_op jit(solution)/shard_map/all_to_all | solution.py:53
  134.2 3.2 reshape.184
  137.5 88.3 %all-to-all-done.1 = bf16[32,512,128]{2,1,0:T(8,128)(2,1)} async-done(((bf16[32,512,128]{2,1,0:T(8,128)(2,1)}), bf16[32,512,128]{2,1,0:T(8,128)(2,1)}, u32[]{:S(2)}, u32[]{:S(2)}) %all-to-all-start.1) | async-done | bytes 4194336 | tf_op jit(solution)/shard_map/all_to_all | solution.py:53
  225.7 2.6 copy.36
  228.4 9.0 %add_convert_fusion = bf16[2,64,128,128]{3,2,1,0:T(8,128)(2,1)S(1)} fusion(bf16[2,64,128,128]{3,2,1,0:T(8,128)(2,1)S(1)} %bitcast.35, f32[64]{0:T(128)S(1)} %multiply_exponential_fusion.2, f32[34,64]{0,1:T(8,128)S(1)} %get-tuple-element.2, bf16[2,34,64,128]{3,2,0,1:T(8,128)(2,1)S(1)} %reshape.184, bf16[2,34,64,128]{3,2,0,1:T(8,128)(2,1)S(1)} %reshape.183), kind=kOutput, calls=%fused_computation.1 | convolution fusion | flops 865140736 | bytes 10625792 | tf_op jit(solution)/shard_map/rsgd,rsge->rgde/dot_general | solution.py:40
  237.4 35.5 %copy.46 = bf16[2,8192,128]{2,0,1:T(2,128)(2,1)} copy(bf16[2,8192,128]{2,1,0:T(8,128)(2,1)S(1)} %bitcast.40) | data formatting | bytes 8388608 | tf_op jit(solution)/shard_map/reshape | solution.py:64
  272.9 4.9 %all-to-all-start.2 = ((bf16[2,8192,128]{2,0,1:T(2,128)(2,1)}), bf16[2,8192,128]{2,0,1:T(2,128)(2,1)}, u32[]{:S(2)}, u32[]{:S(2)}) async-start(bf16[2,8192,128]{2,0,1:T(2,128)(2,1)} %copy.46), calls=%async_computation.2 | async-start | bytes 8388608 | tf_op jit(solution)/shard_map/all_to_all | solution.py:65
  277.8 3.2 reshape.182
  282.9 3.1 fusion
  286.0 1.8 multiply_reduce_fusion
  289.6 2.9 reshape.185
  292.7 3.5 fusion.3
  296.2 74.1 %all-to-all-done.2 = bf16[2,8192,128]{2,0,1:T(2,128)(2,1)} async-done(((bf16[2,8192,128]{2,0,1:T(2,128)(2,1)}), bf16[2,8192,128]{2,0,1:T(2,128)(2,1)}, u32[]{:S(2)}, u32[]{:S(2)}) %all-to-all-start.2) | async-done | bytes 4194336 | tf_op jit(solution)/shard_map/all_to_all | solution.py:65
  370.2 5.2 %copy.47 = bf16[16,2,512,128]{3,2,1,0:T(8,128)(2,1)} copy(bf16[16,2,512,128]{3,1,2,0:T(2,128)(2,1)} %bitcast.9) | data formatting | bytes 8388608 | tf_op jit(solution)/shard_map/all_to_all | solution.py:65
  (35 shorter events, 6.2 us)
Async XLA Ops:
  55.8 6.7 %copy-start.7 = (u32[32]{0:T(128)S(1)}, u32[32]{0:T(128)}, u32[]{:S(2)}) copy-start(u32[32]{0:T(128)} %constant.40) | copy-start | bytes 388
  55.8 7.9 %copy-start.6 = (s32[2]{0:T(128)S(1)}, s32[2]{0:T(128)}, u32[]{:S(2)}) copy-start(s32[2]{0:T(128)} %param.15) | copy-start | bytes 28
  55.8 54.2 %all-to-all-start = ((bf16[16,2,32768]{2,1,0:T(2,128)(2,1)}), bf16[16,2,32768]{2,1,0:T(2,128)(2,1)S(1)}, u32[]{:S(2)}, u32[]{:S(2)}) async-start(bf16[16,2,32768]{2,1,0:T(2,128)(2,1)} %reshape.201), calls=%async_computation | async-start | bytes 4194304 | tf_op jit(solution)/shard_map/all_to_all | solution.py:51
  127.0 6.3 %copy-start.2 = (bf16[2,34,8192]{2,0,1:T(2,128)(2,1)S(1)}, bf16[2,34,8192]{2,0,1:T(2,128)(2,1)}, u32[]{:S(2)}) copy-start(bf16[2,34,8192]{2,0,1:T(2,128)(2,1)} %param.9) | copy-start | bytes 3342340
  127.0 98.8 %all-to-all-start.1 = ((bf16[32,512,128]{2,1,0:T(8,128)(2,1)}), bf16[32,512,128]{2,1,0:T(8,128)(2,1)}, u32[]{:S(2)}, u32[]{:S(2)}) async-start(bf16[32,512,128]{2,1,0:T(8,128)(2,1)} %broadcast_select_fusion), calls=%async_computation.1 | async-start | bytes 8388608 | tf_op jit(solution)/shard_map/all_to_all | solution.py:53
  133.3 4.1 %copy-start.5 = (f32[64]{0:T(128)S(1)}, f32[64]{0:T(128)}, u32[]{:S(2)}) copy-start(f32[64]{0:T(128)} %param.12) | copy-start | bytes 772
  228.4 9.0 %copy-start = (bf16[2,16,512,128]{3,2,1,0:T(8,128)(2,1)}, bf16[2,16,512,128]{3,2,1,0:T(8,128)(2,1)S(1)}, u32[]{:S(2)}) copy-start(bf16[2,16,512,128]{3,2,1,0:T(8,128)(2,1)S(1)} %copy.36) | copy-start | bytes 12582916
  272.9 97.3 %all-to-all-start.2 = ((bf16[2,8192,128]{2,0,1:T(2,128)(2,1)}), bf16[2,8192,128]{2,0,1:T(2,128)(2,1)}, u32[]{:S(2)}, u32[]{:S(2)}) async-start(bf16[2,8192,128]{2,0,1:T(2,128)(2,1)} %copy.46), calls=%async_computation.2 | async-start | bytes 8388608 | tf_op jit(solution)/shard_map/all_to_all | solution.py:65
  282.9 3.1 copy-start.1
  289.6 3.1 copy-start.3
  289.6 3.1 copy-start.4
where the time goes:
time: 376 us; the launch traced here: 375 us
  waiting for transfers between devices  164 us (44%)
  local copies, waits for them, and re-layouts  78.4 us (21%)
  other arithmetic  53.9 us (14%)
  blocking collectives  43.9 us (12%)
  starting transfers between devices  17.8 us (5%)
  matrix products  15.4 us (4%)
    all_to_all x1, waiting for transfers between devices, on_device(): lax.all_to_all(chosen, 'batch', split_axis=0, concat_axis=1, tiled=True)  88.3 us
    all_to_all x1, waiting for transfers between devices, on_device(): lax.all_to_all(local_states, 'batch', split_axis=1, concat_axis=0, tiled=...  74.1 us
    unnamed x1, other arithmetic  45.2 us
    unnamed x1, blocking collectives  43.9 us
    reshape x1, local copies, waits for them, and re-layouts, on_device(): updated.astype(jnp.bfloat16).reshape(req_dev, feature_width, head_size)  35.5 us
    unnamed x24, local copies, waits for them, and re-layouts  20 us
    dot_general x1, matrix products, attend(): jnp.einsum('rsgd,rsge->rgde', weighted_keys, value_wide, precision=highest)  8.99 us
  transfers between devices with their start and end apart: 3, of which 3 were waited for; matrix products, arithmetic and copies ran while one was open for 6% of the time, Pallas kernels for 0%

commit v1 on v0

--- a/solution.py
+++ b/solution.py
@@ -1,6 +1,11 @@
+import functools
+import math
+
 import jax
 import jax.numpy as jnp
 from jax import lax
+from jax.experimental import pallas as pl
+from jax.experimental.pallas import tpu as pltpu
 from jax.sharding import PartitionSpec as P
 
 
@@ -41,12 +46,413 @@
     return (from_state + in_block, updated)
 
 
+MESH = pl.DeviceIdType.MESH
+TILE = 16
+LANES = 128
+
+
+def round_up(count, unit):
+    return -(-count // unit) * unit
+
+
+def plan_rows(rows):
+    padded = round_up(rows, TILE)
+    lead = padded - rows
+    moved = round_up(padded + rows + rows - lead, TILE)
+    return padded, lead, moved
+
+
+def heads_kernel(
+    dims,
+    entry_ref,
+    rates_ref,
+    gain_ref,
+    query_ref,
+    key_ref,
+    value_ref,
+    gate_ref,
+    pool_ref,
+    mixed_ref,
+    new_ref,
+    entry_mine,
+    entry_all,
+    entry_smem,
+    packed,
+    block_all,
+    pool_all,
+    pool_now,
+    att_out,
+    att_in,
+    gated,
+    decay_now,
+    decay_pair,
+    decay_tail,
+    entry_sems,
+    pool_sems,
+    block_sems,
+    att_sems,
+    local_sems,
+):
+    n, reqs, length, heads, head, stride = dims
+    rows = reqs * length
+    padded, lead, moved = plan_rows(rows)
+    part = heads * head
+    width = n * part
+    shift = TILE - lead
+    f32, bf16 = jnp.float32, jnp.bfloat16
+    me = lax.axis_index("batch")
+
+    def target(i):
+        return lax.rem(me + lax.rem(i * stride, n), n)
+
+    def source(i):
+        return lax.rem(me + n - lax.rem(i * stride, n), n)
+
+    barrier = pltpu.get_barrier_semaphore()
+
+    def greet(i, carry):
+        pl.semaphore_signal(barrier, inc=1, device_id={"batch": target(i)}, device_id_type=MESH)
+        return carry
+
+    lax.fori_loop(1, n, greet, 0)
+
+    lane = lax.broadcasted_iota(jnp.int32, (8, LANES), 1)
+    mine = jnp.zeros((8, LANES), jnp.int32)
+    for r in range(reqs):
+        mine = jnp.where(lane == r, entry_ref[r], mine)
+    entry_mine[...] = mine
+    entry_all[me] = mine
+
+    def remote(src, dst, send_sem, recv_sem, peer):
+        return pltpu.make_async_remote_copy(
+            src_ref=src,
+            dst_ref=dst,
+            send_sem=send_sem,
+            recv_sem=recv_sem,
+            device_id={"batch": peer},
+            device_id_type=MESH,
+        )
+
+    def pool_rows(h, peer):
+        return pool_ref.at[0, pl.ds(pl.multiple_of(peer * part + h * head, head), head), :]
+
+    def entry_copy(peer, slot):
+        return remote(
+            entry_mine, entry_all.at[slot], entry_sems.at[0, peer], entry_sems.at[1, slot], peer
+        )
+
+    def pool_copy(h, peer, slot):
+        return remote(
+            pool_rows(h, peer),
+            pool_all.at[h, slot],
+            pool_sems.at[h, 0, peer],
+            pool_sems.at[h, 1, slot],
+            peer,
+        )
+
+    def block_copy(h, peer, slot):
+        return remote(
+            packed.at[h, peer],
+            block_all.at[h, slot],
+            block_sems.at[h, 0, peer],
+            block_sems.at[h, 1, slot],
+            peer,
+        )
+
+    def att_copy(h, peer, slot):
+        return remote(
+            att_out.at[h, peer],
+            att_in.at[h, slot],
+            att_sems.at[h, 0, peer],
+            att_sems.at[h, 1, slot],
+            peer,
+        )
+
+    def own_pool(h):
+        return pltpu.make_async_copy(pool_rows(h, me), pool_all.at[h, me], local_sems.at[0, h])
+
+    def own_att(h):
+        return pltpu.make_async_copy(att_out.at[h, me], att_in.at[h, me], local_sems.at[1, h])
+
+    def block_of(h, peer):
+        cols = pl.ds(pl.multiple_of(peer * part + h * head, head), head)
+        key = key_ref[0:rows, cols].astype(f32)
+        query = query_ref[0:rows, cols].astype(f32)
+        value = value_ref[0:rows, cols].astype(f32)
+        gap = jnp.zeros((moved - 3 * rows, head), f32)
+        return jnp.concatenate([key, query[:lead], value, query[lead:], gap], axis=0).astype(bf16)
+
+    def send_pool(h):
+        def body(i, carry):
+            pool_copy(h, target(i), me).start()
+            return carry
+
+        lax.fori_loop(1, n, body, 0)
+        own_pool(h).start()
+
+    def send_block(h):
+        def body(i, carry):
+            peer = target(i)
+            packed[h, peer] = block_of(h, peer)
+            block_copy(h, peer, me).start()
+            return carry
+
+        lax.fori_loop(1, n, body, 0)
+        block_all[h, me] = block_of(h, me)
+
+    def send_entries(i, carry):
+        entry_copy(target(i), me).start()
+        return carry
+
+    pl.semaphore_wait(barrier, n - 1)
+    lax.fori_loop(1, n, send_entries, 0)
+    ahead = min(2, heads)
+    for h in range(ahead):
+        send_pool(h)
+        send_block(h)
+
+    def time_of(index):
+        return (index // reqs + 1).astype(f32)
+
+    def query_index(shape):
+        row = lax.broadcasted_iota(jnp.int32, shape, 0)
+        return jnp.maximum(jnp.where(row < TILE, row - shift, row - 2 * shift), 0)
+
+    row_q = query_index((padded, head))
+    row_k = lax.broadcasted_iota(jnp.int32, (padded, head), 0)
+    pair_q = query_index((padded, LANES))
+    pair_k = lax.broadcasted_iota(jnp.int32, (padded, LANES), 1)
+    distance = time_of(pair_q) - time_of(pair_k)
+    keep = (distance >= 0.0) & (pair_q % reqs == pair_k % reqs) & (pair_k < rows)
+    for h in range(heads):
+        rate = rates_ref[me * heads + h]
+        decay_now[h] = jnp.exp(-time_of(row_q) * rate)
+        decay_pair[h] = jnp.where(keep, jnp.exp(-jnp.maximum(distance, 0.0) * rate), 0.0)
+        tail = jnp.exp(-jnp.maximum(float(length) - time_of(row_k), 0.0) * rate)
+        for r in range(reqs):
+            decay_tail[h, r] = jnp.where((row_k < rows) & (row_k % reqs == r), tail, 0.0)
+
+    def prepare_gate(j, carry):
+        at = pl.ds(pl.multiple_of(j * part, part), part)
+        gated[:, at] = gain_ref[:, at] * jax.nn.sigmoid(gate_ref[0:rows, at].astype(f32))
+        return carry
+
+    lax.fori_loop(0, n, prepare_gate, 0)
+
+    def wait_entries(i, carry):
+        peer = source(i)
+        entry_copy(peer, peer).wait_recv()
+        return carry
+
+    lax.fori_loop(1, n, wait_entries, 0)
+    listing = pltpu.make_async_copy(entry_all, entry_smem, local_sems.at[2, 0])
+    listing.start()
+    listing.wait()
+
+    def split(wide):
+        high = wide.astype(bf16)
+        return high, (wide - high.astype(f32)).astype(bf16)
+
+    def dot(a, b, dims):
+        return lax.dot_general(a, b, (dims, ((), ())), preferred_element_type=f32)
+
+    def work(h, peer):
+        starts = [pool_now[entry_smem[peer, 0, r]] for r in range(reqs)]
+        key = block_all[h, peer, 0:padded]
+        value = block_all[h, peer, padded : 2 * padded]
+        query = jnp.concatenate(
+            [block_all[h, peer, padded - TILE : padded], block_all[h, peer, 2 * padded - TILE : moved]],
+            axis=0,
+        )
+        from_each = dot(query, jnp.concatenate(starts, axis=1), ((1,), (0,)))
+        from_state = from_each[:, 0:head]
+        for r in range(1, reqs):
+            from_state = jnp.where(
+                row_q % reqs == r, from_each[:, r * head : (r + 1) * head], from_state
+            )
+        scores = dot(query, block_all[h, peer, 0:LANES], ((1,), (1,))) * decay_pair[h]
+        value_long = block_all[h, peer, padded : padded + LANES]
+        attended = from_state * decay_now[h] + dot(
+            jnp.concatenate(split(scores), axis=1),
+            jnp.concatenate([value_long, value_long], axis=0),
+            ((1,), (0,)),
+        )
+        att_out[h, peer, 0:rows] = jnp.concatenate(
+            [attended[shift:TILE], attended[TILE + shift : 2 * shift + rows]], axis=0
+        )
+        value_wide = value.astype(f32)
+        weighted = jnp.concatenate([value_wide * decay_tail[h, r] for r in range(reqs)], axis=1)
+        added = dot(
+            jnp.concatenate([key, key], axis=0),
+            jnp.concatenate(split(weighted), axis=0),
+            ((0,), (0,)),
+        )
+        fade = jnp.exp(jnp.full((8, head), -float(length), f32) * rates_ref[me * heads + h])[0:1]
+        for r in range(reqs):
+            new_ref[peer * reqs + r, pl.ds(pl.multiple_of(h * head, head), head), :] = (
+                fade * starts[r].astype(f32) + added[:, r * head : (r + 1) * head]
+            ).astype(bf16)
+
+    unroll = math.gcd(n, 4)
+
+    def each_head(h, carry):
+        def take_pool(i, inner):
+            peer = source(i)
+            pool_copy(h, peer, peer).wait_recv()
+            pool_now[peer] = pool_all[h, peer]
+            return inner
+
+        own_pool(h).wait()
+        pool_now[me] = pool_all[h, me]
+        lax.fori_loop(1, n, take_pool, 0)
+
+        @pl.when(h + ahead < heads)
+        def _():
+            send_pool(h + ahead)
+            send_block(h + ahead)
+
+        def each_group(g, inner):
+            for u in range(unroll):
+                i = g * unroll + u
+                peer = source(i)
+
+                @pl.when(i > 0)
+                def _():
+                    block_copy(h, peer, peer).wait_recv()
+
+            for u in range(unroll):
+                work(h, source(g * unroll + u))
+            for u in range(unroll):
+                i = g * unroll + u
+                peer = source(i)
+
+                @pl.when(i > 0)
+                def _():
+                    att_copy(h, peer, me).start()
+
+                @pl.when(i == 0)
+                def _():
+                    own_att(h).start()
+
+            return inner
+
+        lax.fori_loop(0, n // unroll, each_group, 0)
+        return carry
+
+    lax.fori_loop(0, heads, each_head, 0)
+
+    def gather_head(h, total):
+        own_att(h).wait()
+        own = att_in[h, me, 0:rows]
+
+        def gather(i, inner):
+            peer = target(i)
+            att_copy(h, peer, peer).wait_recv()
+            here = att_in[h, peer, 0:rows]
+            return inner + here * here
+
+        return lax.fori_loop(1, n, gather, total + own * own)
+
+    squares = lax.fori_loop(0, heads, gather_head, jnp.zeros((rows, head), f32))
+    squares = jnp.sum(squares, axis=1, keepdims=True)
+    scale = lax.rsqrt(squares * (1.0 / width) + 1e-05)
+
+    def finish(j, carry):
+        for h in range(heads):
+            at = pl.ds(pl.multiple_of(j * part + h * head, head), head)
+            mixed_ref[:, at] = (att_in[h, j, 0:rows] * scale * gated[:, at]).astype(bf16)
+        return carry
+
+    lax.fori_loop(0, n, finish, 0)
+
+    def settle(i, carry):
+        peer = target(i)
+        entry_copy(peer, me).wait_send()
+        for h in range(heads):
+            pool_copy(h, peer, me).wait_send()
+            block_copy(h, peer, me).wait_send()
+            att_copy(h, peer, me).wait_send()
+        return carry
+
+    lax.fori_loop(1, n, settle, 0)
+
+
+def by_heads(
+    n, queries, key_vectors, values, gate_logits, decay_rates, norm_gain, pool_states, pool_entry
+):
+    reqs, length, width = queries.shape
+    head = pool_states.shape[2]
+    part = width // n
+    heads = part // head
+    rows = reqs * length
+    padded, lead, moved = plan_rows(rows)
+    sent = round_up(rows, 8)
+    stride = next(s for s in range(max(n // 2 - 1, 1), 0, -1) if math.gcd(s, n) == 1)
+    flat = [
+        item.transpose(1, 0, 2).reshape(rows, width)
+        for item in (queries, key_vectors, values, gate_logits)
+    ]
+    f32, bf16 = jnp.float32, jnp.bfloat16
+    vmem = pl.BlockSpec(memory_space=pltpu.VMEM)
+    smem = pl.BlockSpec(memory_space=pltpu.SMEM)
+    anywhere = pl.BlockSpec(memory_space=pl.ANY)
+    mixed, new_states = pl.pallas_call(
+        functools.partial(heads_kernel, (n, reqs, length, heads, head, stride)),
+        out_shape=(
+            jax.ShapeDtypeStruct((rows, width), bf16),
+            jax.ShapeDtypeStruct((n * reqs, part, head), bf16),
+        ),
+        in_specs=[smem, smem, vmem, vmem, vmem, vmem, vmem, anywhere],
+        out_specs=(vmem, vmem),
+        scratch_shapes=[
+            pltpu.VMEM((8, LANES), jnp.int32),
+            pltpu.VMEM((n, 8, LANES), jnp.int32),
+            pltpu.SMEM((n, 8, LANES), jnp.int32),
+            pltpu.VMEM((heads, n, moved, head), bf16),
+            pltpu.VMEM((heads, n, moved, head), bf16),
+            pltpu.VMEM((heads, n, head, head), bf16),
+            pltpu.VMEM((n, head, head), bf16),
+            pltpu.VMEM((heads, n, sent, head), f32),
+            pltpu.VMEM((heads, n, sent, head), f32),
+            pltpu.VMEM((rows, width), f32),
+            pltpu.VMEM((heads, padded, head), f32),
+            pltpu.VMEM((heads, padded, LANES), f32),
+            pltpu.VMEM((heads, reqs, padded, head), f32),
+            pltpu.SemaphoreType.DMA((2, n)),
+            pltpu.SemaphoreType.DMA((heads, 2, n)),
+            pltpu.SemaphoreType.DMA((heads, 2, n)),
+            pltpu.SemaphoreType.DMA((heads, 2, n)),
+            pltpu.SemaphoreType.DMA((3, heads)),
+        ],
+        compiler_params=pltpu.CompilerParams(
+            collective_id=0, has_side_effects=True, vmem_limit_bytes=44 * 1024 * 1024
+        ),
+    )(pool_entry, decay_rates, norm_gain.reshape(1, width), *flat, pool_states)
+    return mixed.reshape(length, reqs, width).transpose(1, 0, 2), new_states
+
+
 def on_device(
     queries, key_vectors, values, gate_logits, decay_rates, norm_gain, pool_states, pool_entry
 ):
     req_dev, length, feature_width = queries.shape
     head_count = decay_rates.shape[0]
     head_size = pool_states.shape[2]
+    ranks = lax.axis_size("batch")
+    rows = req_dev * length
+    lead = -rows % TILE
+    if (
+        ranks > 1
+        and feature_width % (ranks * head_size) == 0
+        and pool_states.shape[0] == 1
+        and head_size % LANES == 0
+        and 0 < lead < min(rows, TILE)
+        and rows <= LANES
+        and plan_rows(rows)[0] + LANES <= plan_rows(rows)[2]
+        and plan_rows(rows)[2] == 3 * plan_rows(rows)[0] - 2 * TILE
+    ):
+        return by_heads(
+            ranks, queries, key_vectors, values, gate_logits, decay_rates, norm_gain, pool_states, pool_entry
+        )
     entries = lax.all_gather(pool_entry, "batch", axis=0, tiled=True)
     spread = lax.all_to_all(pool_states, "batch", split_axis=1, concat_axis=0, tiled=True)
     chosen = jnp.take(spread, entries, axis=0)

time: 376 us -> 209 us (0.56)
  Pallas kernels: 0 us -> 182 us
  waiting for transfers between devices: 164 us -> 0 us
  local copies, waits for them, and re-layouts: 78.4 us -> 22.6 us
  other arithmetic: 53.9 us -> 0 us
  blocking collectives: 43.9 us -> 0 us
  starting transfers between devices: 17.8 us -> 0 us
  matrix products: 15.4 us -> 0 us
    pallas_call x0 -> x1, Pallas kernels: none -> 182 us  [by_heads(): pl.pallas_call(functools.partial(heads_kernel, (n, reqs, length, heads, h...]
    all_to_all x3 -> x0, waiting for transfers between devices: 164 us -> none  [the longest x1 88.3 us: on_device(): lax.all_to_all(chosen, 'batch', split_axis=0, concat_axis=1, tiled=True)]
    unnamed x1 -> x0, other arithmetic: 45.2 us -> none
    unnamed x1 -> x0, blocking collectives: 43.9 us -> none
    reshape x5, local copies, waits for them, and re-layouts: 45.6 us -> 13.4 us  [the longest x4 9.8 us: by_heads(): item.transpose(1, 0, 2).reshape(rows, width)]
    all_to_all x3 -> x0, starting transfers between devices: 17.8 us -> none  [the longest x1 6.69 us: on_device(): lax.all_to_all(pool_states, 'batch', split_axis=1, concat_axis=0, tiled=T...]
    dot_general x4 -> x0, matrix products: 15.4 us -> none  [the longest x1 8.99 us: attend(): jnp.einsum('rsgd,rsge->rgde', weighted_keys, value_wide, precision=highest)]
    unnamed x24 -> x15, local copies, waits for them, and re-layouts: 20 us -> 9.29 us
  transfers between devices with their start and end apart: 3 -> 0, of which waited for: 3 -> 0; matrix products, arithmetic and copies ran while one was open for 6% -> 0% of each run, Pallas kernels for 0% -> 0%
where the time goes in v1:
time: 209 us; the launch traced here: 205 us
  Pallas kernels  182 us (87%)
  local copies, waits for them, and re-layouts  22.6 us (11%)
    pallas_call x1, Pallas kernels, by_heads(): pl.pallas_call(functools.partial(heads_kernel, (n, reqs, length, heads, h...  182 us
    reshape x4, local copies, waits for them, and re-layouts, by_heads(): item.transpose(1, 0, 2).reshape(rows, width)  9.8 us
    unnamed x15, local copies, waits for them, and re-layouts  9.29 us

profile of v1, /device:TPU:11, one launch (start us, length us, event | category | flops | bytes accessed | tf_op | source)
XLA Modules:
  0.0 205.3 jit_solution(17822131872284156176)
XLA Ops:
  0.6 0.0 copy-start.6
  0.6 2.9 %reshape.23.query_ref = bf16[68,8192]{1,0:T(8,128)(2,1)S(1)} reshape(bf16[34,2,8192]{2,1,0:T(2,128)(2,1)} %bitcast.7) | data formatting | bytes 2228224 | tf_op jit(solution)/shard_map/reshape | solution.py:392
  3.6 0.0 copy-done.6
  3.6 0.4 reshape.24.key_ref
  4.0 2.9 %reshape.25.value_ref = bf16[68,8192]{1,0:T(8,128)(2,1)S(1)} reshape(bf16[34,2,8192]{2,1,0:T(2,128)(2,1)} %bitcast.9) | data formatting | bytes 2228224 | tf_op jit(solution)/shard_map/reshape | solution.py:392
  6.9 0.0 copy-start.4
  6.9 0.0 copy-start.5
  6.9 3.6 %reshape.26.gate_ref = bf16[68,8192]{1,0:T(8,128)(2,1)} reshape(bf16[34,2,8192]{2,1,0:T(2,128)(2,1)} %bitcast.10) | data formatting | bytes 2228224 | tf_op jit(solution)/shard_map/reshape | solution.py:392
  10.5 0.0 copy-done.4
  10.5 0.0 copy-done.5
  10.5 0.0 copy-start
  10.5 1.3 copy-done
  11.8 0.0 copy-start.1
  11.8 1.6 copy-done.1
  13.4 0.0 copy-start.3
  13.4 0.8 copy-done.3
  14.1 181.9 %shard_map.95 = (bf16[68,8192]{1,0:T(8,128)(2,1)S(1)}, bf16[32,512,128]{2,1,0:T(8,128)(2,1)}) custom-call(s32[2]{0:T(128)S(1)} %copy-done.4, f32[64]{0:T(128)S(1)} %copy-done.5, f32[1,8192]{1,0:T(1,128)S(1)} %bitcast.6, bf16[68,8192]{1,0:T(8,128)(2,1)S(1)} %reshape.23.query_ref, bf16[68,8192]{1,0:T(8,128)(2,1)S(1)} %reshape.24.key_ref, ...), custom_call_target="tpu_custom_call" | custom-call | tf_op jit(solution)/shard_map/pallas_call | solution.py:399
  196.0 0.0 copy-start.2
  196.1 1.0 copy-done.2
  197.1 3.6 %reshape.27 = bf16[34,2,8192]{2,1,0:T(2,128)(2,1)} reshape(bf16[68,8192]{1,0:T(8,128)(2,1)} %copy-done.2) | data formatting | bytes 2228224 | tf_op jit(solution)/shard_map/reshape | solution.py:431
  200.6 4.7 %copy.11 = bf16[32,512,128]{2,1,0:T(8,128)(2,1)} copy(bf16[32,512,128]{2,1,0:T(8,128)(2,1)} %get-tuple-element.9) | data formatting | bytes 8388608
Async XLA Ops:
  0.6 3.0 %copy-start.6 = (bf16[2,34,8192]{2,0,1:T(2,128)(2,1)S(1)}, bf16[2,34,8192]{2,0,1:T(2,128)(2,1)}, u32[]{:S(2)}) copy-start(bf16[2,34,8192]{2,0,1:T(2,128)(2,1)} %param.9) | copy-start | bytes 3342340
  6.9 3.6 %copy-start.4 = (s32[2]{0:T(128)S(1)}, s32[2]{0:T(128)}, u32[]{:S(2)}) copy-start(s32[2]{0:T(128)} %entry_ref.1) | copy-start | bytes 28
  6.9 3.6 %copy-start.5 = (f32[64]{0:T(128)S(1)}, f32[64]{0:T(128)}, u32[]{:S(2)}) copy-start(f32[64]{0:T(128)} %rates_ref.1) | copy-start | bytes 772
  10.5 1.3 copy-start
  11.8 1.6 copy-start.1
  13.4 0.8 copy-start.3
  196.0 1.0 copy-start.2

commit v2 on v1

--- a/solution.py
+++ b/solution.py
@@ -93,7 +93,7 @@
     att_sems,
     local_sems,
 ):
-    n, reqs, length, heads, head, stride = dims
+    n, reqs, length, heads, head = dims
     rows = reqs * length
     padded, lead, moved = plan_rows(rows)
     part = heads * head
@@ -102,16 +102,19 @@
     f32, bf16 = jnp.float32, jnp.bfloat16
     me = lax.axis_index("batch")
 
-    def target(i):
-        return lax.rem(me + lax.rem(i * stride, n), n)
-
-    def source(i):
-        return lax.rem(me + n - lax.rem(i * stride, n), n)
+    def partner(i):
+        step = (i % 2) * (n // 2) + i // 2
+        peer = 0
+        bit = 1
+        while bit < n:
+            peer = peer + ((me // bit + step // bit) % 2) * bit
+            bit *= 2
+        return peer
 
     barrier = pltpu.get_barrier_semaphore()
 
     def greet(i, carry):
-        pl.semaphore_signal(barrier, inc=1, device_id={"batch": target(i)}, device_id_type=MESH)
+        pl.semaphore_signal(barrier, inc=1, device_id={"batch": partner(i)}, device_id_type=MESH)
         return carry
 
     lax.fori_loop(1, n, greet, 0)
@@ -184,7 +187,7 @@
 
     def send_pool(h):
         def body(i, carry):
-            pool_copy(h, target(i), me).start()
+            pool_copy(h, partner(i), me).start()
             return carry
 
         lax.fori_loop(1, n, body, 0)
@@ -192,7 +195,7 @@
 
     def send_block(h):
         def body(i, carry):
-            peer = target(i)
+            peer = partner(i)
             packed[h, peer] = block_of(h, peer)
             block_copy(h, peer, me).start()
             return carry
@@ -201,7 +204,7 @@
         block_all[h, me] = block_of(h, me)
 
     def send_entries(i, carry):
-        entry_copy(target(i), me).start()
+        entry_copy(partner(i), me).start()
         return carry
 
     pl.semaphore_wait(barrier, n - 1)
@@ -240,7 +243,7 @@
     lax.fori_loop(0, n, prepare_gate, 0)
 
     def wait_entries(i, carry):
-        peer = source(i)
+        peer = partner(i)
         entry_copy(peer, peer).wait_recv()
         return carry
 
@@ -297,7 +300,7 @@
 
     def each_head(h, carry):
         def take_pool(i, inner):
-            peer = source(i)
+            peer = partner(i)
             pool_copy(h, peer, peer).wait_recv()
             pool_now[peer] = pool_all[h, peer]
             return inner
@@ -314,17 +317,17 @@
         def each_group(g, inner):
             for u in range(unroll):
                 i = g * unroll + u
-                peer = source(i)
+                peer = partner(i)
 
                 @pl.when(i > 0)
                 def _():
                     block_copy(h, peer, peer).wait_recv()
 
             for u in range(unroll):
-                work(h, source(g * unroll + u))
+                work(h, partner(g * unroll + u))
             for u in range(unroll):
                 i = g * unroll + u
-                peer = source(i)
+                peer = partner(i)
 
                 @pl.when(i > 0)
                 def _():
@@ -346,7 +349,7 @@
         own = att_in[h, me, 0:rows]
 
         def gather(i, inner):
-            peer = target(i)
+            peer = partner(i)
             att_copy(h, peer, peer).wait_recv()
             here = att_in[h, peer, 0:rows]
             return inner + here * here
@@ -366,7 +369,7 @@
     lax.fori_loop(0, n, finish, 0)
 
     def settle(i, carry):
-        peer = target(i)
+        peer = partner(i)
         entry_copy(peer, me).wait_send()
         for h in range(heads):
             pool_copy(h, peer, me).wait_send()
@@ -387,7 +390,6 @@
     rows = reqs * length
     padded, lead, moved = plan_rows(rows)
     sent = round_up(rows, 8)
-    stride = next(s for s in range(max(n // 2 - 1, 1), 0, -1) if math.gcd(s, n) == 1)
     flat = [
         item.transpose(1, 0, 2).reshape(rows, width)
         for item in (queries, key_vectors, values, gate_logits)
@@ -397,7 +399,7 @@
     smem = pl.BlockSpec(memory_space=pltpu.SMEM)
     anywhere = pl.BlockSpec(memory_space=pl.ANY)
     mixed, new_states = pl.pallas_call(
-        functools.partial(heads_kernel, (n, reqs, length, heads, head, stride)),
+        functools.partial(heads_kernel, (n, reqs, length, heads, head)),
         out_shape=(
             jax.ShapeDtypeStruct((rows, width), bf16),
             jax.ShapeDtypeStruct((n * reqs, part, head), bf16),
@@ -442,6 +444,7 @@
     lead = -rows % TILE
     if (
         ranks > 1
+        and ranks & (ranks - 1) == 0
         and feature_width % (ranks * head_size) == 0
         and pool_states.shape[0] == 1
         and head_size % LANES == 0

time: 209 us -> 208 us (level); the launches traced: 205 us -> 207 us
  no operation moved by 1% of the time
where the time goes in v2:
time: 208 us; the launch traced here: 207 us
  Pallas kernels  184 us (88%)
  local copies, waits for them, and re-layouts  22.6 us (11%)
    pallas_call x1, Pallas kernels, by_heads(): pl.pallas_call(functools.partial(heads_kernel, (n, reqs, length, heads, h...  184 us
    reshape x4, local copies, waits for them, and re-layouts, by_heads(): item.transpose(1, 0, 2).reshape(rows, width)  9.8 us
    unnamed x15, local copies, waits for them, and re-layouts  9.29 us

profile of v2, /device:TPU:11, one launch (start us, length us, event | category | flops | bytes accessed | tf_op | source)
XLA Modules:
  0.0 207.0 jit_solution(6719432960320708971)
XLA Ops:
  0.6 0.0 copy-start.6
  0.6 2.9 %reshape.23.query_ref = bf16[68,8192]{1,0:T(8,128)(2,1)S(1)} reshape(bf16[34,2,8192]{2,1,0:T(2,128)(2,1)} %bitcast.7) | data formatting | bytes 2228224 | tf_op jit(solution)/shard_map/reshape | solution.py:394
  3.6 0.0 copy-done.6
  3.6 0.4 reshape.24.key_ref
  4.0 2.9 %reshape.25.value_ref = bf16[68,8192]{1,0:T(8,128)(2,1)S(1)} reshape(bf16[34,2,8192]{2,1,0:T(2,128)(2,1)} %bitcast.9) | data formatting | bytes 2228224 | tf_op jit(solution)/shard_map/reshape | solution.py:394
  6.9 0.0 copy-start.4
  6.9 0.0 copy-start.5
  6.9 3.6 %reshape.26.gate_ref = bf16[68,8192]{1,0:T(8,128)(2,1)} reshape(bf16[34,2,8192]{2,1,0:T(2,128)(2,1)} %bitcast.10) | data formatting | bytes 2228224 | tf_op jit(solution)/shard_map/reshape | solution.py:394
  10.5 0.0 copy-done.4
  10.5 0.0 copy-done.5
  10.5 0.0 copy-start
  10.5 1.3 copy-done
  11.8 0.0 copy-start.1
  11.8 1.6 copy-done.1
  13.4 0.0 copy-start.3
  13.4 0.8 copy-done.3
  14.1 183.7 %shard_map.95 = (bf16[68,8192]{1,0:T(8,128)(2,1)S(1)}, bf16[32,512,128]{2,1,0:T(8,128)(2,1)}) custom-call(s32[2]{0:T(128)S(1)} %copy-done.4, f32[64]{0:T(128)S(1)} %copy-done.5, f32[1,8192]{1,0:T(1,128)S(1)} %bitcast.6, bf16[68,8192]{1,0:T(8,128)(2,1)S(1)} %reshape.23.query_ref, bf16[68,8192]{1,0:T(8,128)(2,1)S(1)} %reshape.24.key_ref, ...), custom_call_target="tpu_custom_call" | custom-call | tf_op jit(solution)/shard_map/pallas_call | solution.py:401
  197.8 0.0 copy-start.2
  197.8 1.0 copy-done.2
  198.8 3.6 %reshape.27 = bf16[34,2,8192]{2,1,0:T(2,128)(2,1)} reshape(bf16[68,8192]{1,0:T(8,128)(2,1)} %copy-done.2) | data formatting | bytes 2228224 | tf_op jit(solution)/shard_map/reshape | solution.py:433
  202.4 4.7 %copy.11 = bf16[32,512,128]{2,1,0:T(8,128)(2,1)} copy(bf16[32,512,128]{2,1,0:T(8,128)(2,1)} %get-tuple-element.9) | data formatting | bytes 8388608
Async XLA Ops:
  0.6 3.0 %copy-start.6 = (bf16[2,34,8192]{2,0,1:T(2,128)(2,1)S(1)}, bf16[2,34,8192]{2,0,1:T(2,128)(2,1)}, u32[]{:S(2)}) copy-start(bf16[2,34,8192]{2,0,1:T(2,128)(2,1)} %param.9) | copy-start | bytes 3342340
  6.9 3.6 %copy-start.4 = (s32[2]{0:T(128)S(1)}, s32[2]{0:T(128)}, u32[]{:S(2)}) copy-start(s32[2]{0:T(128)} %entry_ref.1) | copy-start | bytes 28
  6.9 3.6 %copy-start.5 = (f32[64]{0:T(128)S(1)}, f32[64]{0:T(128)}, u32[]{:S(2)}) copy-start(f32[64]{0:T(128)} %rates_ref.1) | copy-start | bytes 772
  10.5 1.3 copy-start
  11.8 1.6 copy-start.1
  13.4 0.8 copy-start.3
  197.8 1.0 copy-start.2

commit v3 on v2

--- a/solution.py
+++ b/solution.py
@@ -49,6 +49,7 @@
 MESH = pl.DeviceIdType.MESH
 TILE = 16
 LANES = 128
+CODE_TOP = 32000.0
 
 
 def round_up(count, unit):
@@ -83,6 +84,7 @@
     pool_now,
     att_out,
     att_in,
+    att_wide,
     gated,
     decay_now,
     decay_pair,
@@ -259,6 +261,24 @@
     def dot(a, b, dims):
         return lax.dot_general(a, b, (dims, ((), ())), preferred_element_type=f32)
 
+    code_row = lax.broadcasted_iota(jnp.int32, (padded, head), 0)
+    code_col = lax.broadcasted_iota(jnp.int32, (padded, head), 1)
+
+    def encode(wide):
+        size = jnp.abs(wide)
+        power = jnp.ceil(jnp.log2(jnp.maximum(jnp.max(size, axis=1, keepdims=True), 1e-30)))
+        root = jnp.sqrt(size * jnp.exp2(-power)) * CODE_TOP
+        code = jnp.where(wide < 0.0, -root, root)
+        powers = jnp.sum(jnp.where(code_row == code_col, power, 0.0), axis=0, keepdims=True)
+        code = jnp.where(code_row == rows, powers, code)
+        return jnp.round(code).astype(jnp.int32).astype(jnp.int16)
+
+    def decode(code):
+        wide = code.astype(jnp.int32).astype(f32)
+        powers = jnp.where(code_row == code_col, wide[rows : rows + 1], 0.0)
+        power = jnp.exp2(jnp.sum(powers, axis=1, keepdims=True)) * (1.0 / (CODE_TOP * CODE_TOP))
+        return (wide * jnp.abs(wide) * power)[0:rows]
+
     def work(h, peer):
         starts = [pool_now[entry_smem[peer, 0, r]] for r in range(reqs)]
         key = block_all[h, peer, 0:padded]
@@ -280,8 +300,15 @@
             jnp.concatenate([value_long, value_long], axis=0),
             ((1,), (0,)),
         )
-        att_out[h, peer, 0:rows] = jnp.concatenate(
-            [attended[shift:TILE], attended[TILE + shift : 2 * shift + rows]], axis=0
+        att_out[h, peer] = encode(
+            jnp.concatenate(
+                [
+                    attended[shift:TILE],
+                    attended[TILE + shift : 2 * shift + rows],
+                    jnp.zeros((padded - rows, head), f32),
+                ],
+                axis=0,
+            )
         )
         value_wide = value.astype(f32)
         weighted = jnp.concatenate([value_wide * decay_tail[h, r] for r in range(reqs)], axis=1)
@@ -346,12 +373,14 @@
 
     def gather_head(h, total):
         own_att(h).wait()
-        own = att_in[h, me, 0:rows]
+        own = decode(att_in[h, me])
+        att_wide[h, me] = own
 
         def gather(i, inner):
             peer = partner(i)
             att_copy(h, peer, peer).wait_recv()
-            here = att_in[h, peer, 0:rows]
+            here = decode(att_in[h, peer])
+            att_wide[h, peer] = here
             return inner + here * here
 
         return lax.fori_loop(1, n, gather, total + own * own)
@@ -363,7 +392,7 @@
     def finish(j, carry):
         for h in range(heads):
             at = pl.ds(pl.multiple_of(j * part + h * head, head), head)
-            mixed_ref[:, at] = (att_in[h, j, 0:rows] * scale * gated[:, at]).astype(bf16)
+            mixed_ref[:, at] = (att_wide[h, j] * scale * gated[:, at]).astype(bf16)
         return carry
 
     lax.fori_loop(0, n, finish, 0)
@@ -389,7 +418,6 @@
     heads = part // head
     rows = reqs * length
     padded, lead, moved = plan_rows(rows)
-    sent = round_up(rows, 8)
     flat = [
         item.transpose(1, 0, 2).reshape(rows, width)
         for item in (queries, key_vectors, values, gate_logits)
@@ -414,8 +442,9 @@
             pltpu.VMEM((heads, n, moved, head), bf16),
             pltpu.VMEM((heads, n, head, head), bf16),
             pltpu.VMEM((n, head, head), bf16),
-            pltpu.VMEM((heads, n, sent, head), f32),
-            pltpu.VMEM((heads, n, sent, head), f32),
+            pltpu.VMEM((heads, n, padded, head), jnp.int16),
+            pltpu.VMEM((heads, n, padded, head), jnp.int16),
+            pltpu.VMEM((heads, n, rows, head), f32),
             pltpu.VMEM((rows, width), f32),
             pltpu.VMEM((heads, padded, head), f32),
             pltpu.VMEM((heads, padded, LANES), f32),

time: 208 us -> 187 us (0.90)
  Pallas kernels: 184 us -> 161 us
    pallas_call x1, Pallas kernels: 184 us -> 161 us  [by_heads(): pl.pallas_call(functools.partial(heads_kernel, (n, reqs, length, heads, h...]
where the time goes in v3:
time: 187 us; the launch traced here: 185 us
  Pallas kernels  161 us (86%)
  local copies, waits for them, and re-layouts  22.6 us (12%)
    pallas_call x1, Pallas kernels, by_heads(): pl.pallas_call(functools.partial(heads_kernel, (n, reqs, length, heads, h...  161 us
    reshape x4, local copies, waits for them, and re-layouts, by_heads(): item.transpose(1, 0, 2).reshape(rows, width)  9.8 us
    unnamed x15, local copies, waits for them, and re-layouts  9.29 us

profile of v3, /device:TPU:11, one launch (start us, length us, event | category | flops | bytes accessed | tf_op | source)
XLA Modules:
  0.0 184.7 jit_solution(818921966306805537)
XLA Ops:
  0.6 0.0 copy-start.6
  0.6 2.9 %reshape.23.query_ref = bf16[68,8192]{1,0:T(8,128)(2,1)S(1)} reshape(bf16[34,2,8192]{2,1,0:T(2,128)(2,1)} %bitcast.7) | data formatting | bytes 2228224 | tf_op jit(solution)/shard_map/reshape | solution.py:422
  3.6 0.0 copy-done.6
  3.6 0.4 reshape.24.key_ref
  4.0 2.9 %reshape.25.value_ref = bf16[68,8192]{1,0:T(8,128)(2,1)S(1)} reshape(bf16[34,2,8192]{2,1,0:T(2,128)(2,1)} %bitcast.9) | data formatting | bytes 2228224 | tf_op jit(solution)/shard_map/reshape | solution.py:422
  6.9 0.0 copy-start.4
  6.9 0.0 copy-start.5
  6.9 3.6 %reshape.26.gate_ref = bf16[68,8192]{1,0:T(8,128)(2,1)} reshape(bf16[34,2,8192]{2,1,0:T(2,128)(2,1)} %bitcast.10) | data formatting | bytes 2228224 | tf_op jit(solution)/shard_map/reshape | solution.py:422
  10.5 0.0 copy-done.4
  10.5 0.0 copy-done.5
  10.5 0.0 copy-start
  10.5 1.3 copy-done
  11.8 0.0 copy-start.1
  11.8 1.6 copy-done.1
  13.4 0.0 copy-start.3
  13.4 0.8 copy-done.3
  14.1 161.3 %shard_map.95 = (bf16[68,8192]{1,0:T(8,128)(2,1)S(1)}, bf16[32,512,128]{2,1,0:T(8,128)(2,1)}) custom-call(s32[2]{0:T(128)S(1)} %copy-done.4, f32[64]{0:T(128)S(1)} %copy-done.5, f32[1,8192]{1,0:T(1,128)S(1)} %bitcast.6, bf16[68,8192]{1,0:T(8,128)(2,1)S(1)} %reshape.23.query_ref, bf16[68,8192]{1,0:T(8,128)(2,1)S(1)} %reshape.24.key_ref, ...), custom_call_target="tpu_custom_call" | custom-call | tf_op jit(solution)/shard_map/pallas_call | solution.py:429
  175.4 0.0 copy-start.2
  175.4 1.0 copy-done.2
  176.5 3.6 %reshape.27 = bf16[34,2,8192]{2,1,0:T(2,128)(2,1)} reshape(bf16[68,8192]{1,0:T(8,128)(2,1)} %copy-done.2) | data formatting | bytes 2228224 | tf_op jit(solution)/shard_map/reshape | solution.py:462
  180.0 4.7 %copy.11 = bf16[32,512,128]{2,1,0:T(8,128)(2,1)} copy(bf16[32,512,128]{2,1,0:T(8,128)(2,1)} %get-tuple-element.9) | data formatting | bytes 8388608
Async XLA Ops:
  0.6 3.0 %copy-start.6 = (bf16[2,34,8192]{2,0,1:T(2,128)(2,1)S(1)}, bf16[2,34,8192]{2,0,1:T(2,128)(2,1)}, u32[]{:S(2)}) copy-start(bf16[2,34,8192]{2,0,1:T(2,128)(2,1)} %param.9) | copy-start | bytes 3342340
  6.9 3.6 %copy-start.4 = (s32[2]{0:T(128)S(1)}, s32[2]{0:T(128)}, u32[]{:S(2)}) copy-start(s32[2]{0:T(128)} %entry_ref.1) | copy-start | bytes 28
  6.9 3.6 %copy-start.5 = (f32[64]{0:T(128)S(1)}, f32[64]{0:T(128)}, u32[]{:S(2)}) copy-start(f32[64]{0:T(128)} %rates_ref.1) | copy-start | bytes 772
  10.5 1.3 copy-start
  11.8 1.6 copy-start.1
  13.4 0.8 copy-start.3
  175.4 1.0 copy-start.2

commit v4 on v3

--- a/solution.py
+++ b/solution.py
@@ -75,6 +75,7 @@
     pool_ref,
     mixed_ref,
     new_ref,
+    staged,
     entry_mine,
     entry_all,
     entry_smem,
@@ -93,6 +94,7 @@
     pool_sems,
     block_sems,
     att_sems,
+    state_sems,
     local_sems,
 ):
     n, reqs, length, heads, head = dims
@@ -179,6 +181,15 @@
     def own_att(h):
         return pltpu.make_async_copy(att_out.at[h, me], att_in.at[h, me], local_sems.at[1, h])
 
+    def states_copy(h, peer):
+        return pltpu.make_async_copy(
+            staged.at[h, peer],
+            new_ref.at[
+                pl.ds(peer * reqs, reqs), pl.ds(pl.multiple_of(h * head, head), head), :
+            ],
+            state_sems.at[h, peer],
+        )
+
     def block_of(h, peer):
         cols = pl.ds(pl.multiple_of(peer * part + h * head, head), head)
         key = key_ref[0:rows, cols].astype(f32)
@@ -195,26 +206,35 @@
         lax.fori_loop(1, n, body, 0)
         own_pool(h).start()
 
-    def send_block(h):
+    def pack_block(h, peer):
+        packed[h, peer] = block_of(h, peer)
+
+    def send_block(h, ready):
         def body(i, carry):
             peer = partner(i)
-            packed[h, peer] = block_of(h, peer)
+            if not ready:
+                pack_block(h, peer)
             block_copy(h, peer, me).start()
             return carry
 
         lax.fori_loop(1, n, body, 0)
         block_all[h, me] = block_of(h, me)
 
+    def pack_first(i, carry):
+        pack_block(0, partner(i))
+        return carry
+
+    lax.fori_loop(1, n, pack_first, 0)
+
     def send_entries(i, carry):
         entry_copy(partner(i), me).start()
         return carry
 
     pl.semaphore_wait(barrier, n - 1)
     lax.fori_loop(1, n, send_entries, 0)
-    ahead = min(2, heads)
-    for h in range(ahead):
+    for h in range(heads):
         send_pool(h)
-        send_block(h)
+        send_block(h, h == 0)
 
     def time_of(index):
         return (index // reqs + 1).astype(f32)
@@ -319,7 +339,7 @@
         )
         fade = jnp.exp(jnp.full((8, head), -float(length), f32) * rates_ref[me * heads + h])[0:1]
         for r in range(reqs):
-            new_ref[peer * reqs + r, pl.ds(pl.multiple_of(h * head, head), head), :] = (
+            staged[h, peer, r] = (
                 fade * starts[r].astype(f32) + added[:, r * head : (r + 1) * head]
             ).astype(bf16)
 
@@ -336,11 +356,6 @@
         pool_now[me] = pool_all[h, me]
         lax.fori_loop(1, n, take_pool, 0)
 
-        @pl.when(h + ahead < heads)
-        def _():
-            send_pool(h + ahead)
-            send_block(h + ahead)
-
         def each_group(g, inner):
             for u in range(unroll):
                 i = g * unroll + u
@@ -364,6 +379,7 @@
                 def _():
                     own_att(h).start()
 
+                states_copy(h, peer).start()
             return inner
 
         lax.fori_loop(0, n // unroll, each_group, 0)
@@ -404,9 +420,12 @@
             pool_copy(h, peer, me).wait_send()
             block_copy(h, peer, me).wait_send()
             att_copy(h, peer, me).wait_send()
+            states_copy(h, peer).wait()
         return carry
 
     lax.fori_loop(1, n, settle, 0)
+    for h in range(heads):
+        states_copy(h, me).wait()
 
 
 def by_heads(
@@ -433,8 +452,9 @@
             jax.ShapeDtypeStruct((n * reqs, part, head), bf16),
         ),
         in_specs=[smem, smem, vmem, vmem, vmem, vmem, vmem, anywhere],
-        out_specs=(vmem, vmem),
+        out_specs=(vmem, anywhere),
         scratch_shapes=[
+            pltpu.VMEM((heads, n, reqs, head, head), bf16),
             pltpu.VMEM((8, LANES), jnp.int32),
             pltpu.VMEM((n, 8, LANES), jnp.int32),
             pltpu.SMEM((n, 8, LANES), jnp.int32),
@@ -453,10 +473,11 @@
             pltpu.SemaphoreType.DMA((heads, 2, n)),
             pltpu.SemaphoreType.DMA((heads, 2, n)),
             pltpu.SemaphoreType.DMA((heads, 2, n)),
+            pltpu.SemaphoreType.DMA((heads, n)),
             pltpu.SemaphoreType.DMA((3, heads)),
         ],
         compiler_params=pltpu.CompilerParams(
-            collective_id=0, has_side_effects=True, vmem_limit_bytes=44 * 1024 * 1024
+            collective_id=0, has_side_effects=True, vmem_limit_bytes=38 * 1024 * 1024
         ),
     )(pool_entry, decay_rates, norm_gain.reshape(1, width), *flat, pool_states)
     return mixed.reshape(length, reqs, width).transpose(1, 0, 2), new_states

time: 187 us -> 188 us (level)
  local copies, waits for them, and re-layouts: 22.6 us -> 24.6 us
    unnamed x15 -> x17, local copies, waits for them, and re-layouts: 9.29 us -> 11.2 us
where the time goes in v4:
time: 188 us; the launch traced here: 185 us
  Pallas kernels  160 us (85%)
  local copies, waits for them, and re-layouts  24.6 us (13%)
    pallas_call x1, Pallas kernels, by_heads(): pl.pallas_call(functools.partial(heads_kernel, (n, reqs, length, heads, h...  160 us
    unnamed x17, local copies, waits for them, and re-layouts  11.2 us
    reshape x4, local copies, waits for them, and re-layouts, by_heads(): item.transpose(1, 0, 2).reshape(rows, width)  9.8 us

profile of v4, /device:TPU:11, one launch (start us, length us, event | category | flops | bytes accessed | tf_op | source)
XLA Modules:
  0.0 185.2 jit_solution(3744903473427732912)
XLA Ops:
  0.6 0.0 copy-start.7
  0.6 2.9 %reshape.23.query_ref = bf16[68,8192]{1,0:T(8,128)(2,1)S(1)} reshape(bf16[34,2,8192]{2,1,0:T(2,128)(2,1)} %bitcast.7) | data formatting | bytes 2228224 | tf_op jit(solution)/shard_map/reshape | solution.py:441
  3.6 0.0 copy-done.7
  3.6 0.4 reshape.24.key_ref
  4.0 2.9 %reshape.25.value_ref = bf16[68,8192]{1,0:T(8,128)(2,1)S(1)} reshape(bf16[34,2,8192]{2,1,0:T(2,128)(2,1)} %bitcast.9) | data formatting | bytes 2228224 | tf_op jit(solution)/shard_map/reshape | solution.py:441
  6.9 0.0 copy-start.5
  6.9 0.0 copy-start.6
  6.9 3.6 %reshape.26.gate_ref = bf16[68,8192]{1,0:T(8,128)(2,1)} reshape(bf16[34,2,8192]{2,1,0:T(2,128)(2,1)} %bitcast.10) | data formatting | bytes 2228224 | tf_op jit(solution)/shard_map/reshape | solution.py:441
  10.5 0.0 copy-done.5
  10.5 0.0 copy-done.6
  10.5 0.0 copy-start
  10.5 1.3 copy-done
  11.8 0.0 copy-start.2
  11.8 1.6 copy-done.2
  13.4 0.0 copy-start.4
  13.4 0.8 copy-done.4
  14.1 159.9 %shard_map.95 = (bf16[68,8192]{1,0:T(8,128)(2,1)S(1)}, bf16[32,512,128]{2,1,0:T(8,128)(2,1)S(1)}) custom-call(s32[2]{0:T(128)S(1)} %copy-done.5, f32[64]{0:T(128)S(1)} %copy-done.6, f32[1,8192]{1,0:T(1,128)S(1)} %bitcast.6, bf16[68,8192]{1,0:T(8,128)(2,1)S(1)} %reshape.23.query_ref, bf16[68,8192]{1,0:T(8,128)(2,1)S(1)} %reshape.24.key_ref, ...), custom_call_target="tpu_custom_call" | custom-call | tf_op jit(solution)/shard_map/pallas_call | solution.py:448
  174.0 0.0 copy-start.1
  174.0 1.9 %copy-done.1 = bf16[32,512,128]{2,1,0:T(8,128)(2,1)} copy-done((bf16[32,512,128]{2,1,0:T(8,128)(2,1)}, bf16[32,512,128]{2,1,0:T(8,128)(2,1)S(1)}, u32[]{:S(2)}) %copy-start.1) | copy-done | bytes 4194328
  176.0 0.0 copy-start.3
  176.0 1.0 copy-done.3
  177.0 3.6 %reshape.27 = bf16[34,2,8192]{2,1,0:T(2,128)(2,1)} reshape(bf16[68,8192]{1,0:T(8,128)(2,1)} %copy-done.3) | data formatting | bytes 2228224 | tf_op jit(solution)/shard_map/reshape | solution.py:483
  180.5 4.7 %copy.11 = bf16[32,512,128]{2,1,0:T(8,128)(2,1)} copy(bf16[32,512,128]{2,1,0:T(8,128)(2,1)} %copy-done.1) | data formatting | bytes 8388608
Async XLA Ops:
  0.6 3.0 %copy-start.7 = (bf16[2,34,8192]{2,0,1:T(2,128)(2,1)S(1)}, bf16[2,34,8192]{2,0,1:T(2,128)(2,1)}, u32[]{:S(2)}) copy-start(bf16[2,34,8192]{2,0,1:T(2,128)(2,1)} %param.9) | copy-start | bytes 3342340
  6.9 3.6 %copy-start.5 = (s32[2]{0:T(128)S(1)}, s32[2]{0:T(128)}, u32[]{:S(2)}) copy-start(s32[2]{0:T(128)} %entry_ref.1) | copy-start | bytes 28
  6.9 3.6 %copy-start.6 = (f32[64]{0:T(128)S(1)}, f32[64]{0:T(128)}, u32[]{:S(2)}) copy-start(f32[64]{0:T(128)} %rates_ref.1) | copy-start | bytes 772
  10.5 1.3 copy-start
  11.8 1.6 copy-start.2
  13.4 0.8 copy-start.4
  174.0 1.9 %copy-start.1 = (bf16[32,512,128]{2,1,0:T(8,128)(2,1)}, bf16[32,512,128]{2,1,0:T(8,128)(2,1)S(1)}, u32[]{:S(2)}) copy-start(bf16[32,512,128]{2,1,0:T(8,128)(2,1)S(1)} %get-tuple-element.9) | copy-start | bytes 12582916
  176.0 1.0 copy-start.3

commit v5 on v4

--- a/solution.py
+++ b/solution.py
@@ -209,16 +209,18 @@
     def pack_block(h, peer):
         packed[h, peer] = block_of(h, peer)
 
-    def send_block(h, ready):
+    def send_block(h, first, last, ready):
         def body(i, carry):
-            peer = partner(i)
-            if not ready:
-                pack_block(h, peer)
-            block_copy(h, peer, me).start()
+            @pl.when(i > 0)
+            def _():
+                peer = partner(i)
+                if not ready:
+                    pack_block(h, peer)
+                block_copy(h, peer, me).start()
+
             return carry
 
-        lax.fori_loop(1, n, body, 0)
-        block_all[h, me] = block_of(h, me)
+        lax.fori_loop(first, last, body, 0)
 
     def pack_first(i, carry):
         pack_block(0, partner(i))
@@ -232,9 +234,10 @@
 
     pl.semaphore_wait(barrier, n - 1)
     lax.fori_loop(1, n, send_entries, 0)
+    send_pool(0)
+    send_block(0, 0, n, True)
     for h in range(heads):
-        send_pool(h)
-        send_block(h, h == 0)
+        block_all[h, me] = block_of(h, me)
 
     def time_of(index):
         return (index // reqs + 1).astype(f32)
@@ -356,6 +359,10 @@
         pool_now[me] = pool_all[h, me]
         lax.fori_loop(1, n, take_pool, 0)
 
+        @pl.when(h + 1 < heads)
+        def _():
+            send_pool(h + 1)
+
         def each_group(g, inner):
             for u in range(unroll):
                 i = g * unroll + u
@@ -364,6 +371,10 @@
                 @pl.when(i > 0)
                 def _():
                     block_copy(h, peer, peer).wait_recv()
+
+            @pl.when(h + 1 < heads)
+            def _():
+                send_block(h + 1, g * unroll, (g + 1) * unroll, False)
 
             for u in range(unroll):
                 work(h, partner(g * unroll + u))
@@ -380,6 +391,7 @@
                     own_att(h).start()
 
                 states_copy(h, peer).start()
+
             return inner
 
         lax.fori_loop(0, n // unroll, each_group, 0)

time: 188 us -> 192 us (1.021)
  Pallas kernels: 160 us -> 165 us
    pallas_call x1, Pallas kernels: 160 us -> 165 us  [by_heads(): pl.pallas_call(functools.partial(heads_kernel, (n, reqs, length, heads, h...]
where the time goes in v5:
time: 192 us; the launch traced here: 191 us
  Pallas kernels  165 us (86%)
  local copies, waits for them, and re-layouts  24.6 us (13%)
    pallas_call x1, Pallas kernels, by_heads(): pl.pallas_call(functools.partial(heads_kernel, (n, reqs, length, heads, h...  165 us
    unnamed x17, local copies, waits for them, and re-layouts  11.2 us
    reshape x4, local copies, waits for them, and re-layouts, by_heads(): item.transpose(1, 0, 2).reshape(rows, width)  9.8 us

profile of v5, /device:TPU:11, one launch (start us, length us, event | category | flops | bytes accessed | tf_op | source)
XLA Modules:
  0.0 190.6 jit_solution(9554172215111274592)
XLA Ops:
  0.6 0.0 copy-start.7
  0.6 2.9 %reshape.23.query_ref = bf16[68,8192]{1,0:T(8,128)(2,1)S(1)} reshape(bf16[34,2,8192]{2,1,0:T(2,128)(2,1)} %bitcast.7) | data formatting | bytes 2228224 | tf_op jit(solution)/shard_map/reshape | solution.py:453
  3.6 0.0 copy-done.7
  3.6 0.4 reshape.24.key_ref
  4.0 2.9 %reshape.25.value_ref = bf16[68,8192]{1,0:T(8,128)(2,1)S(1)} reshape(bf16[34,2,8192]{2,1,0:T(2,128)(2,1)} %bitcast.9) | data formatting | bytes 2228224 | tf_op jit(solution)/shard_map/reshape | solution.py:453
  6.9 0.0 copy-start.5
  6.9 0.0 copy-start.6
  6.9 3.6 %reshape.26.gate_ref = bf16[68,8192]{1,0:T(8,128)(2,1)} reshape(bf16[34,2,8192]{2,1,0:T(2,128)(2,1)} %bitcast.10) | data formatting | bytes 2228224 | tf_op jit(solution)/shard_map/reshape | solution.py:453
  10.5 0.0 copy-done.5
  10.5 0.0 copy-done.6
  10.5 0.0 copy-start
  10.5 1.3 copy-done
  11.8 0.0 copy-start.2
  11.8 1.6 copy-done.2
  13.4 0.0 copy-start.4
  13.4 0.8 copy-done.4
  14.1 165.3 %shard_map.95 = (bf16[68,8192]{1,0:T(8,128)(2,1)S(1)}, bf16[32,512,128]{2,1,0:T(8,128)(2,1)S(1)}) custom-call(s32[2]{0:T(128)S(1)} %copy-done.5, f32[64]{0:T(128)S(1)} %copy-done.6, f32[1,8192]{1,0:T(1,128)S(1)} %bitcast.6, bf16[68,8192]{1,0:T(8,128)(2,1)S(1)} %reshape.23.query_ref, bf16[68,8192]{1,0:T(8,128)(2,1)S(1)} %reshape.24.key_ref, ...), custom_call_target="tpu_custom_call" | custom-call | tf_op jit(solution)/shard_map/pallas_call | solution.py:460
  179.5 0.0 copy-start.1
  179.5 1.9 %copy-done.1 = bf16[32,512,128]{2,1,0:T(8,128)(2,1)} copy-done((bf16[32,512,128]{2,1,0:T(8,128)(2,1)}, bf16[32,512,128]{2,1,0:T(8,128)(2,1)S(1)}, u32[]{:S(2)}) %copy-start.1) | copy-done | bytes 4194328
  181.4 0.0 copy-start.3
  181.4 1.0 copy-done.3
  182.4 3.6 %reshape.27 = bf16[34,2,8192]{2,1,0:T(2,128)(2,1)} reshape(bf16[68,8192]{1,0:T(8,128)(2,1)} %copy-done.3) | data formatting | bytes 2228224 | tf_op jit(solution)/shard_map/reshape | solution.py:495
  186.0 4.7 %copy.11 = bf16[32,512,128]{2,1,0:T(8,128)(2,1)} copy(bf16[32,512,128]{2,1,0:T(8,128)(2,1)} %copy-done.1) | data formatting | bytes 8388608
Async XLA Ops:
  0.6 3.0 %copy-start.7 = (bf16[2,34,8192]{2,0,1:T(2,128)(2,1)S(1)}, bf16[2,34,8192]{2,0,1:T(2,128)(2,1)}, u32[]{:S(2)}) copy-start(bf16[2,34,8192]{2,0,1:T(2,128)(2,1)} %param.9) | copy-start | bytes 3342340
  6.9 3.6 %copy-start.5 = (s32[2]{0:T(128)S(1)}, s32[2]{0:T(128)}, u32[]{:S(2)}) copy-start(s32[2]{0:T(128)} %entry_ref.1) | copy-start | bytes 28
  6.9 3.6 %copy-start.6 = (f32[64]{0:T(128)S(1)}, f32[64]{0:T(128)}, u32[]{:S(2)}) copy-start(f32[64]{0:T(128)} %rates_ref.1) | copy-start | bytes 772
  10.5 1.3 copy-start
  11.8 1.6 copy-start.2
  13.4 0.8 copy-start.4
  179.5 1.9 %copy-start.1 = (bf16[32,512,128]{2,1,0:T(8,128)(2,1)}, bf16[32,512,128]{2,1,0:T(8,128)(2,1)S(1)}, u32[]{:S(2)}) copy-start(bf16[32,512,128]{2,1,0:T(8,128)(2,1)S(1)} %get-tuple-element.9) | copy-start | bytes 12582916
  181.4 1.0 copy-start.3

commit v6 on v4

--- a/solution.py
+++ b/solution.py
@@ -192,9 +192,9 @@
 
     def block_of(h, peer):
         cols = pl.ds(pl.multiple_of(peer * part + h * head, head), head)
-        key = key_ref[0:rows, cols].astype(f32)
-        query = query_ref[0:rows, cols].astype(f32)
-        value = value_ref[0:rows, cols].astype(f32)
+        key, query, value = (
+            ref[:, :, cols].astype(f32).reshape(rows, head) for ref in (key_ref, query_ref, value_ref)
+        )
         gap = jnp.zeros((moved - 3 * rows, head), f32)
         return jnp.concatenate([key, query[:lead], value, query[lead:], gap], axis=0).astype(bf16)
 
@@ -259,7 +259,8 @@
 
     def prepare_gate(j, carry):
         at = pl.ds(pl.multiple_of(j * part, part), part)
-        gated[:, at] = gain_ref[:, at] * jax.nn.sigmoid(gate_ref[0:rows, at].astype(f32))
+        gate = gate_ref[:, :, at].astype(f32).reshape(rows, part)
+        gated[:, at] = gain_ref[:, at] * jax.nn.sigmoid(gate)
         return carry
 
     lax.fori_loop(0, n, prepare_gate, 0)
@@ -408,7 +409,8 @@
     def finish(j, carry):
         for h in range(heads):
             at = pl.ds(pl.multiple_of(j * part + h * head, head), head)
-            mixed_ref[:, at] = (att_wide[h, j] * scale * gated[:, at]).astype(bf16)
+            done = att_wide[h, j] * scale * gated[:, at]
+            mixed_ref[:, :, at] = done.reshape(length, reqs, head).astype(bf16)
         return carry
 
     lax.fori_loop(0, n, finish, 0)
@@ -438,8 +440,7 @@
     rows = reqs * length
     padded, lead, moved = plan_rows(rows)
     flat = [
-        item.transpose(1, 0, 2).reshape(rows, width)
-        for item in (queries, key_vectors, values, gate_logits)
+        item.transpose(1, 0, 2) for item in (queries, key_vectors, values, gate_logits)
     ]
     f32, bf16 = jnp.float32, jnp.bfloat16
     vmem = pl.BlockSpec(memory_space=pltpu.VMEM)
@@ -448,7 +449,7 @@
     mixed, new_states = pl.pallas_call(
         functools.partial(heads_kernel, (n, reqs, length, heads, head)),
         out_shape=(
-            jax.ShapeDtypeStruct((rows, width), bf16),
+            jax.ShapeDtypeStruct((length, reqs, width), bf16),
             jax.ShapeDtypeStruct((n * reqs, part, head), bf16),
         ),
         in_specs=[smem, smem, vmem, vmem, vmem, vmem, vmem, anywhere],
@@ -480,7 +481,7 @@
             collective_id=0, has_side_effects=True, vmem_limit_bytes=38 * 1024 * 1024
         ),
     )(pool_entry, decay_rates, norm_gain.reshape(1, width), *flat, pool_states)
-    return mixed.reshape(length, reqs, width).transpose(1, 0, 2), new_states
+    return mixed.transpose(1, 0, 2), new_states
 
 
 def on_device(

time: 188 us -> 176 us (0.936)
  local copies, waits for them, and re-layouts: 24.6 us -> 11.6 us
    reshape x5 -> x0, local copies, waits for them, and re-layouts: 13.4 us -> none  [the longest x4 9.8 us: by_heads(): item.transpose(1, 0, 2).reshape(rows, width)]
    unnamed x17 -> x18, local copies, waits for them, and re-layouts: 11.2 us -> 11.6 us
where the time goes in v6:
time: 176 us; the launch traced here: 173 us
  Pallas kernels  161 us (91%)
  local copies, waits for them, and re-layouts  11.6 us (7%)
    pallas_call x1, Pallas kernels, by_heads(): pl.pallas_call(functools.partial(heads_kernel, (n, reqs, length, heads, h...  161 us
    unnamed x18, local copies, waits for them, and re-layouts  11.6 us

profile of v6, /device:TPU:11, one launch (start us, length us, event | category | flops | bytes accessed | tf_op | source)
XLA Modules:
  0.0 173.3 jit_solution(16552381058506431226)
XLA Ops:
  0.6 0.0 copy-start
  0.6 1.6 copy-done
  2.2 0.0 copy-start.1
  2.2 1.2 copy-done.1
  3.5 0.0 copy-start.2
  3.5 1.2 copy-done.2
  4.7 0.0 copy-start.3
  4.7 1.2 copy-done.3
  6.0 0.0 copy-start.4
  6.0 1.2 copy-done.4
  7.2 0.0 copy-start.5
  7.2 0.8 copy-done.5
  8.0 0.0 copy-start.6
  8.0 0.7 copy-done.6
  8.6 0.0 copy-start.7
  8.6 0.7 copy-done.7
  9.3 161.0 %shard_map.95 = (bf16[34,2,8192]{2,1,0:T(2,128)(2,1)S(1)}, bf16[32,512,128]{2,1,0:T(8,128)(2,1)S(1)}) custom-call(s32[2]{0:T(128)S(1)} %copy-done.6, f32[64]{0:T(128)S(1)} %copy-done.7, f32[1,8192]{1,0:T(1,128)S(1)} %bitcast.11, bf16[34,2,8192]{2,1,0:T(2,128)(2,1)S(1)} %bitcast.6, bf16[34,2,8192]{2,1,0:T(2,128)(2,1)S(1)} %bitcast.7, ...), custom_call_target="tpu_custom_call" | custom-call | tf_op jit(solution)/shard_map/pallas_call | solution.py:449
  170.3 1.0 copy.12
  171.3 2.0 %copy.13 = bf16[32,512,128]{2,1,0:T(8,128)(2,1)} copy(bf16[32,512,128]{2,1,0:T(8,128)(2,1)S(1)} %get-tuple-element.9) | data formatting | bytes 8388608
Async XLA Ops:
  0.6 1.6 copy-start
  2.2 1.2 copy-start.1
  3.5 1.2 copy-start.2
  4.7 1.2 copy-start.3
  6.0 1.2 copy-start.4
  7.2 0.8 copy-start.5
  8.0 0.7 copy-start.6
  8.6 0.7 copy-start.7

commit v7 on v6

--- a/solution.py
+++ b/solution.py
@@ -344,6 +344,21 @@
                 fade * starts[r].astype(f32) + added[:, r * head : (r + 1) * head]
             ).astype(bf16)
 
+    def gather_head(h, total):
+        own_att(h).wait()
+        own = decode(att_in[h, me])
+        att_wide[h, me] = own
+
+        def gather(i, inner):
+            peer = partner(i)
+            att_copy(h, peer, peer).wait_recv()
+            here = decode(att_in[h, peer])
+            att_wide[h, peer] = here
+            return inner + here * here
+
+        return lax.fori_loop(1, n, gather, total + own * own)
+
+    lag = min(2, heads)
     unroll = math.gcd(n, 4)
 
     def each_head(h, carry):
@@ -384,25 +399,11 @@
             return inner
 
         lax.fori_loop(0, n // unroll, each_group, 0)
-        return carry
-
-    lax.fori_loop(0, heads, each_head, 0)
-
-    def gather_head(h, total):
-        own_att(h).wait()
-        own = decode(att_in[h, me])
-        att_wide[h, me] = own
-
-        def gather(i, inner):
-            peer = partner(i)
-            att_copy(h, peer, peer).wait_recv()
-            here = decode(att_in[h, peer])
-            att_wide[h, peer] = here
-            return inner + here * here
-
-        return lax.fori_loop(1, n, gather, total + own * own)
-
-    squares = lax.fori_loop(0, heads, gather_head, jnp.zeros((rows, head), f32))
+        return lax.cond(h >= lag, lambda total: gather_head(h - lag, total), lambda total: total, carry)
+
+    squares = lax.fori_loop(0, heads, each_head, jnp.zeros((rows, head), f32))
+
+    squares = lax.fori_loop(heads - lag, heads, gather_head, squares)
     squares = jnp.sum(squares, axis=1, keepdims=True)
     scale = lax.rsqrt(squares * (1.0 / width) + 1e-05)
 

time: 176 us -> 176 us (level)
  no operation moved by 1% of the time
where the time goes in v7:
time: 176 us; the launch traced here: 173 us
  Pallas kernels  161 us (91%)
  local copies, waits for them, and re-layouts  11.6 us (7%)
    pallas_call x1, Pallas kernels, by_heads(): pl.pallas_call(functools.partial(heads_kernel, (n, reqs, length, heads, h...  161 us
    unnamed x18, local copies, waits for them, and re-layouts  11.6 us

profile of v7, /device:TPU:11, one launch (start us, length us, event | category | flops | bytes accessed | tf_op | source)
XLA Modules:
  0.0 173.3 jit_solution(11678739871030909996)
XLA Ops:
  0.6 0.0 copy-start
  0.6 1.6 copy-done
  2.2 0.0 copy-start.1
  2.2 1.2 copy-done.1
  3.5 0.0 copy-start.2
  3.5 1.2 copy-done.2
  4.7 0.0 copy-start.3
  4.7 1.2 copy-done.3
  6.0 0.0 copy-start.4
  6.0 1.2 copy-done.4
  7.2 0.0 copy-start.5
  7.2 0.8 copy-done.5
  8.0 0.0 copy-start.6
  8.0 0.7 copy-done.6
  8.6 0.0 copy-start.7
  8.6 0.7 copy-done.7
  9.3 161.0 %shard_map.95 = (bf16[34,2,8192]{2,1,0:T(2,128)(2,1)S(1)}, bf16[32,512,128]{2,1,0:T(8,128)(2,1)S(1)}) custom-call(s32[2]{0:T(128)S(1)} %copy-done.6, f32[64]{0:T(128)S(1)} %copy-done.7, f32[1,8192]{1,0:T(1,128)S(1)} %bitcast.11, bf16[34,2,8192]{2,1,0:T(2,128)(2,1)S(1)} %bitcast.6, bf16[34,2,8192]{2,1,0:T(2,128)(2,1)S(1)} %bitcast.7, ...), custom_call_target="tpu_custom_call" | custom-call | tf_op jit(solution)/shard_map/pallas_call | solution.py:450
  170.3 1.0 copy.12
  171.3 2.0 %copy.13 = bf16[32,512,128]{2,1,0:T(8,128)(2,1)} copy(bf16[32,512,128]{2,1,0:T(8,128)(2,1)S(1)} %get-tuple-element.9) | data formatting | bytes 8388608
Async XLA Ops:
  0.6 1.6 copy-start
  2.2 1.2 copy-start.1
  3.5 1.2 copy-start.2
  4.7 1.2 copy-start.3
  6.0 1.2 copy-start.4
  7.2 0.8 copy-start.5
  8.0 0.7 copy-start.6
  8.6 0.7 copy-start.7
